TPU v7x, 512 devices: a whole 4x4x16 slice. The times are simulated.
512 devices in a mesh: grp: 32 (over y, x, core), seq: 16 (over z).
Axes of the slice: x: 4, y: 4, z: 16, core: 2. Of those that a mesh axis runs over, the one named last changes fastest.
Arguments:
- query_sp: bfloat16 [32, 16, 256, 1536], P('grp', 'seq'), may hold values from -80 to 80
- key_sp: bfloat16 [32, 16, 256, 1536], P('grp', 'seq'), may hold values from -8 to 8
- value_sp: bfloat16 [32, 16, 256, 1536], P('grp', 'seq'), may hold values from -6 to 6
- query_tm: bfloat16 [32, 16, 256, 1536], P('grp', 'seq'), may hold values from -80 to 80
- key_tm: bfloat16 [32, 16, 256, 1536], P('grp', 'seq'), may hold values from -8 to 8
- clip_shape: int32 [32, 2], replicated, may hold values from 1 to 256, as said below
- route: int32 [32], replicated, may hold values from 0 to 31
Outputs:
- mixed: bfloat16 [32, 16, 256, 1536], P('grp', 'seq')
Inputs may be any that keep to these rules, and one draw needn't show every extreme that they name: `clip_shape`: each entry of column 0 is one of 4, 8, 16; each entry of column 1 is a multiple of 64 up to 256; clip 0 has 16 frames and 256 patches.
All inputs are finite; a program needn't handle non-finite values.
Results may differ from a plain program's by a relative error of at most 0.015.
Values may be sent and summed in bfloat16 or wider, within the bound.
A program may use at most 64 MiB of HBM per device.

v0:
```python
import functools

import jax
import jax.numpy as jnp
from jax import lax
from jax.experimental import pallas as pl
from jax.experimental.pallas import tpu as pltpu
from jax.sharding import PartitionSpec as P

HD = 128
TILE = 16
MESH = pl.DeviceIdType.MESH
NEG = -1e30
PLANS = (
    ((6, 11, 5), (3, 2, 17), (1, 2, 21)),
    ((6, 12, 6), (3, 2, 19), (2, 1, 34)),
    ((4, 13, 7), (2, 2, 18), (1, 1, 23)),
)


def capacity(plan):
    sums = []
    for _, count, slots in plan:
        sums.append(count * slots + (sums[-1] if sums else 0))
    return sums


def swapped(value, axis, bit):
    mask = 2**bit
    pairs = [(source, source ^ mask) for source in range(lax.axis_size(axis))]
    return lax.ppermute(value, axis, pairs)


def softmax_rows(scores):
    top = jnp.max(scores, axis=-1, keepdims=True)
    expo = jnp.exp(scores - top)
    return expo / jnp.sum(expo, axis=-1, keepdims=True)


def section_cross(route, group_idx, section):
    partner = jnp.bitwise_xor(group_idx, 1 << section)
    lower = jnp.minimum(group_idx, partner)
    return jnp.bitwise_and(jnp.right_shift(route[lower], section), 1) == 1


def general(query_sp, key_sp, value_sp, query_tm, key_tm, clip_shape, route):
    groups = lax.axis_size("grp")
    shards = lax.axis_size("seq")
    group_idx = lax.axis_index("grp")
    shard_idx = lax.axis_index("seq")
    sections = groups.bit_length() - 1
    frames_dev = query_sp.shape[1]
    patches = query_sp.shape[2]
    width = query_sp.shape[3]
    heads = width // HD
    frames = frames_dev * shards
    patches_dev = patches // shards
    scale = HD ** (-0.5)
    own_shape = clip_shape[group_idx]
    frame_ids = shard_idx * frames_dev + jnp.arange(frames_dev, dtype=jnp.int32)
    patch_all = jnp.arange(patches, dtype=jnp.int32)
    shaped = (frames_dev, patches, heads, HD)
    queries = query_sp[0].reshape(shaped)
    keys = key_sp[0].reshape(shaped)
    values = value_sp[0].reshape(shaped)
    scores = (
        jnp.einsum("fphd,fqhd->fhpq", queries, keys, preferred_element_type=jnp.float32) * scale
    )
    scores = jnp.where(patch_all[None, None, None, :] < own_shape[1], scores, NEG)
    weights = softmax_rows(scores).astype(jnp.bfloat16)
    spatial = jnp.einsum("fhpq,fqhd->fphd", weights, values, preferred_element_type=jnp.float32)
    valid_sp = (frame_ids[:, None] < own_shape[0]) & (patch_all[None, :] < own_shape[1])
    spatial = jnp.where(valid_sp[:, :, None, None], spatial, 0.0).astype(jnp.bfloat16)
    spatial = spatial.reshape(1, frames_dev, patches, width)
    query_pt, key_pt, spatial_pt = (
        lax.all_to_all(query_tm, "seq", split_axis=2, concat_axis=1, tiled=True),
        lax.all_to_all(key_tm, "seq", split_axis=2, concat_axis=1, tiled=True),
        lax.all_to_all(spatial, "seq", split_axis=2, concat_axis=1, tiled=True),
    )
    frame_all = jnp.arange(frames, dtype=jnp.int32)
    patch_ids = shard_idx * patches_dev + jnp.arange(patches_dev, dtype=jnp.int32)
    shaped_tm = (frames, patches_dev, heads, HD)
    queries_tm = query_pt[0].reshape(shaped_tm)
    keys_tm = key_pt[0].reshape(shaped_tm)
    values_tm = spatial_pt[0].reshape(shaped_tm)
    scores_tm = (
        jnp.einsum("fphd,gphd->phfg", queries_tm, keys_tm, preferred_element_type=jnp.float32)
        * scale
    )
    scores_tm = jnp.where(frame_all[None, None, None, :] < own_shape[0], scores_tm, NEG)
    weights_tm = softmax_rows(scores_tm).astype(jnp.bfloat16)
    temporal = jnp.einsum(
        "phfg,gphd->fphd", weights_tm, values_tm, preferred_element_type=jnp.float32
    )
    valid_tm = (frame_all[:, None] < own_shape[0]) & (patch_ids[None, :] < own_shape[1])
    temporal = jnp.where(valid_tm[:, :, None, None], temporal, 0.0).astype(jnp.bfloat16)
    temporal = temporal.reshape(1, frames, patches_dev, width)
    result = lax.all_to_all(temporal, "seq", split_axis=1, concat_axis=2, tiled=True)
    for section in range(sections):
        other = swapped(result, "grp", section)
        result = jnp.where(section_cross(route, group_idx, section), other, result)
    return result


def softmax_weights(scores):
    top = jnp.max(scores, axis=-1, keepdims=True)
    expo = jnp.exp(scores - top)
    return (expo * (1.0 / jnp.sum(expo, axis=-1, keepdims=True))).astype(jnp.bfloat16)


def nt_dot(a, b):
    return lax.dot_general(a, b, (((1,), (1,)), ((), ())), preferred_element_type=jnp.float32)


def kernel(
    plan, shape_ref, route_ref,
    q_hbm, k_hbm, v_hbm, qt_hbm, kt_hbm, o_ref,
    inp, xs, xr0, xr1, xr2, zs16, zq16, oz16, zs8, zq8, oz8, zs4, zq4, oz4, wts, bias, zr, xso, xro,
    table, slot_ref, first, units, out_tab,
    in_sem, xss, xrs, xls, zss, zrs, zls, tab_sem,
):
    total = capacity(plan)[-1]
    c = lax.axis_index("grp")
    z = lax.axis_index("seq")
    core = lax.rem(c, 2)
    xr = (xr0, xr1, xr2)
    barrier = pltpu.get_barrier_semaphore()

    def greet_x(d, _):
        pl.semaphore_signal(barrier, inc=1, device_id={"grp": lax.rem(c + d, 32)}, device_id_type=MESH)
        return 0

    def greet_z(d, _):
        pl.semaphore_signal(barrier, inc=1, device_id={"seq": lax.rem(z + d, 16)}, device_id_type=MESH)
        return 0

    lax.fori_loop(1, 16, greet_z, 0)
    lax.fori_loop(1, 32, greet_x, 0)

    loads = [
        pltpu.make_async_copy(ref.at[0, 0], inp.at[i], in_sem.at[i])
        for i, ref in enumerate((kt_hbm, qt_hbm, q_hbm, k_hbm, v_hbm))
    ]
    for load in loads:
        load.start()

    def pack(a):
        def group(s, _):
            for hg in range(4):
                for t in range(12):
                    b, m = divmod(t, 3)
                    rows = pl.ds(pl.multiple_of(64 * b + 16 * s, 16), 16)
                    lanes = pl.ds((3 * hg + m) * HD, HD)
                    dev = 2 * (4 * s + hg) + lax.rem(t + core, 2)
                    xs[a, dev, t // 2] = inp[a, rows, lanes]
            return 0

        lax.fori_loop(0, 4, group, 0)

    def x_send(src, dst, i):
        def one(d, _):
            other = d >= 15
            e = jnp.where(other, d - 15, jnp.where(d >= 10, d + 1, d))
            row, col = lax.rem(e // 4 + 2 + c // 8, 4), lax.rem(lax.rem(e, 4) + 2 + lax.rem(c // 2, 4), 4)
            dev = 8 * row + 2 * col + lax.rem(core + jnp.where(other, 1, 0), 2)
            pltpu.make_async_remote_copy(
                src_ref=src.at[dev], dst_ref=dst.at[c], send_sem=xss.at[i], recv_sem=xrs.at[i],
                device_id={"grp": dev}, device_id_type=MESH,
            ).start()
            return 0

        lax.fori_loop(0, 31, one, 0)
        pltpu.make_async_copy(src.at[c], dst.at[c], xls.at[i]).start()

    def x_wait(src, dst, i):
        part = dst.at[pl.ds(0, 31)]
        pltpu.make_async_copy(part, part, xrs.at[i]).wait()
        pltpu.make_async_copy(src.at[c], dst.at[c], xls.at[i]).wait()

    def x_drain(src, i):
        part = src.at[pl.ds(0, 31)]
        pltpu.make_async_copy(part, part, xss.at[i]).wait()

    loads[0].wait()
    pack(0)
    pl.semaphore_wait(barrier, 46)
    x_send(xs.at[0], xr[0], 0)
    loads[1].wait()
    pack(1)
    x_send(xs.at[1], xr[1], 1)

    def count_units(clip, sums):
        frames = shape_ref[0, clip]
        count = (3 * (shape_ref[1, clip] >> 6) + 1 - ((core + clip) & 1)) >> 1
        units[clip] = count
        is16, is8 = frames == 16, frames == 8
        first[clip] = jnp.where(is16, sums[0], jnp.where(is8, sums[1], sums[2]))
        return (
            sums[0] + jnp.where(is16, count, 0),
            sums[1] + jnp.where(is8, count, 0),
            sums[2] + jnp.where(is16 | is8, 0, count),
        )

    zero = jnp.int32(0)
    n16, n8, _ = lax.fori_loop(0, 32, count_units, (zero, zero, zero))

    row = lax.broadcasted_iota(jnp.int32, table.shape[1:], 0)
    lane = lax.broadcasted_iota(jnp.int32, table.shape[1:], 1)
    place = 128 * row + lane

    def find_slots(clip, found):
        unit, count = found
        frames = shape_ref[0, clip]
        start = first[clip] + jnp.where(frames == 16, 0, jnp.where(frames == 8, n16, n16 + n8))
        first[clip] = start
        inner = place - start
        hit = (inner >= 0) & (inner < units[clip])
        return jnp.where(hit, inner + 6 * clip, unit), jnp.where(hit, frames, count)

    unit, count = lax.fori_loop(0, 32, find_slots, (jnp.zeros_like(place), jnp.full_like(place, 16)))
    table[0] = unit
    table[1] = count
    to_smem = pltpu.make_async_copy(table, slot_ref, tab_sem.at[0])
    to_smem.start()

    row_id = lax.broadcasted_iota(jnp.int32, (256, 256), 0)
    col_id = lax.broadcasted_iota(jnp.int32, (256, 256), 1)
    for i in range(3):
        period = 16 * 2**i
        same = (row_id & (period - 1)) == (col_id & (period - 1))
        bias[i] = jnp.where(same, 0.0, NEG)
    zr[total] = jnp.zeros((TILE, HD), jnp.bfloat16)

    for i in (2, 3, 4):
        loads[i].wait()
    scale = HD ** (-0.5)
    lane_id = lax.broadcasted_iota(jnp.int32, (1, 256), 1)
    key_bias = jnp.where(lane_id < shape_ref[1, c], 0.0, NEG)

    def heads(hg, _):
        for m in range(3):
            lanes = pl.ds(pl.multiple_of((3 * hg + m) * HD, HD), HD)
            scores = nt_dot(inp[2, :, lanes], inp[3, :, lanes]) * scale + key_bias
            weights = softmax_weights(scores)
            out = jnp.dot(weights, inp[4, :, lanes], preferred_element_type=jnp.float32)
            out = out.astype(jnp.bfloat16)
            for b in range(4):
                t = 3 * b + m
                for s in range(4):
                    dev = 2 * (4 * s + hg) + lax.rem(t + core, 2)
                    xs[2, dev, t // 2] = out[64 * b + 16 * s : 64 * b + 16 * s + 16]
        return 0

    lax.fori_loop(0, 4, heads, 0)
    x_send(xs.at[2], xr[2], 2)
    to_smem.wait()

    class Ring:
        def __init__(self, kind, sources, send, land, back):
            self.kind, self.sources, self.send, self.land, self.back = kind, sources, send, land, back
            self.start, self.count, self.slots = plan[kind]
            self.off = capacity(plan)[kind] - self.count * self.slots
            self.place = lax.rem(z - self.start + 16, 16)
            self.works = self.place < self.count

    rings = (Ring(0, 16, zs16, zq16, oz16), Ring(1, 8, zs8, zq8, oz8), Ring(2, 4, zs4, zq4, oz4))

    def entry(kind, r):
        return slot_ref[kind, r >> 7, r & 127]

    def on_sources(ring, run):
        if ring.sources == 16:
            run()
        else:
            pl.when(z < ring.sources)(run)

    def z_send(a, ring):
        i = 3 * a + ring.kind

        def one(d, _):
            j = lax.rem(z + d, ring.count)
            dev = lax.rem(ring.start + j, 16)
            for k in range(ring.slots):
                index = entry(0, ring.off + j * ring.slots + k)
                ring.send[a, j, k] = xr[a][index // 6, lax.rem(index, 6)]

            @pl.when(dev != z)
            def _():
                pltpu.make_async_remote_copy(
                    src_ref=ring.send.at[a, j], dst_ref=ring.land.at[a, z], send_sem=zss.at[i], recv_sem=zrs.at[i],
                    device_id={"seq": dev}, device_id_type=MESH,
                ).start()

            @pl.when(dev == z)
            def _():
                pltpu.make_async_copy(ring.send.at[a, j], ring.land.at[a, z], zls.at[i]).start()

            return 0

        lax.fori_loop(0, ring.count, one, 0)

    def z_sent(a, ring):
        i = 3 * a + ring.kind
        for mine in (0, 1):
            if ring.count > mine:

                @pl.when(ring.works if mine else jnp.logical_not(ring.works))
                def _():
                    part = ring.send.at[a, pl.ds(0, ring.count - mine)]
                    pltpu.make_async_copy(part, part, zss.at[i]).wait()

    def z_wait(a, ring):
        i = 3 * a + ring.kind
        part = ring.land.at[a, pl.ds(0, ring.sources - 1)]
        pltpu.make_async_copy(part, part, zrs.at[i]).wait()
        one = ring.land.at[a, 0]
        pltpu.make_async_copy(one, one, zls.at[i]).wait()

    for a in range(3):
        x_wait(xs.at[a], xr[a], a)
        for ring in rings:
            on_sources(ring, functools.partial(z_send, a, ring))

    def trace(group):
        for b in reversed(range(5)):
            low = group & (31 - (1 << b))
            group = group ^ (((route_ref[low] >> b) & 1) << b)
        return group

    def route_units(group, _):
        clip = trace(group)
        start = first[clip]
        count = jnp.where(z < shape_ref[0, clip], units[clip], 0)
        for i in range(6):
            out_tab[group * 6 + i] = jnp.where(i < count, start + i, total)
        return 0

    lax.fori_loop(0, 32, route_units, 0)

    for ring in rings:
        step = 16 // ring.sources
        ring.blocks = [(k, min(step, ring.slots - k), k // step) for k in range(0, ring.slots, step)]

    def block(ring, a, k, n):
        return ring.land[a, :, k : k + n].reshape(ring.sources * n * TILE, HD)

    def z_weights(ring):
        for a in range(2):
            z_wait(a, ring)
        for k, n, at in ring.blocks:
            rows = ring.sources * n * TILE
            scores = nt_dot(block(ring, 1, k, n), block(ring, 0, k, n)) * scale
            which = {1: 0, 2: 1, 4: 2}.get(n)
            if which is None:
                r = lax.broadcasted_iota(jnp.int32, (rows, rows), 0)
                q = lax.broadcasted_iota(jnp.int32, (rows, rows), 1)
                scores = jnp.where(lax.rem(r, n * TILE) == lax.rem(q, n * TILE), scores, NEG)
            else:
                scores = scores + bias[which, :rows, :rows]
            if ring.kind < 2:
                lane = lax.broadcasted_iota(jnp.int32, (1, rows), 1)
                frame = lane // (n * TILE)
                spot = ring.off + ring.place * ring.slots + k
                count = entry(1, spot)
                if n == 2:
                    count = jnp.where((lane // TILE) % 2 == 0, count, entry(1, spot + 1))
                scores = scores + jnp.where(frame < count, 0.0, NEG)
            wts[ring.kind, at, :rows, :rows] = softmax_weights(scores)

    def z_values(ring):
        z_wait(2, ring)
        for k, n, at in ring.blocks:
            rows = ring.sources * n * TILE
            out = jnp.dot(
                wts[ring.kind, at, :rows, :rows], block(ring, 2, k, n), preferred_element_type=jnp.float32
            ).astype(jnp.bfloat16)
            out = out.reshape(ring.sources, n, TILE, HD)
            for j in range(n):
                ring.back[:, k + j] = out[:, j]
        i = 9 + ring.kind
        home = zr.at[pl.ds(ring.off + ring.place * ring.slots, ring.slots)]

        def one(d, _):
            dev = lax.rem(z + d, ring.sources)
            pltpu.make_async_remote_copy(
                src_ref=ring.back.at[dev], dst_ref=home, send_sem=zss.at[i], recv_sem=zrs.at[i],
                device_id={"seq": dev}, device_id_type=MESH,
            ).start()
            return 0

        lax.fori_loop(1, ring.sources, one, 0)
        pltpu.make_async_copy(ring.back.at[z], home, zls.at[i]).start()

    def z_home(ring):
        i = 9 + ring.kind
        for mine in (0, 1):

            @pl.when(ring.works if mine else jnp.logical_not(ring.works))
            def _():
                if ring.count > mine:
                    part = zr.at[pl.ds(ring.off, (ring.count - mine) * ring.slots)]
                    pltpu.make_async_copy(part, part, zrs.at[i]).wait()
                if mine:
                    one = ring.back.at[0]
                    pltpu.make_async_copy(one, one, zls.at[i]).wait()

    def z_returned(ring):
        part = ring.back.at[pl.ds(0, ring.sources - 1)]
        pltpu.make_async_copy(part, part, zss.at[9 + ring.kind]).wait()

    for ring in rings:
        pl.when(ring.works)(functools.partial(z_weights, ring))
    for ring in rings:
        pl.when(ring.works)(functools.partial(z_values, ring))
    for ring in rings:
        on_sources(ring, functools.partial(z_home, ring))

    def collect(dev, _):
        for i in range(6):
            xso[dev, i] = zr[out_tab[dev * 6 + i]]
        return 0

    lax.fori_loop(0, 32, collect, 0)
    x_send(xso, xro, 3)
    x_wait(xso, xro, 3)
    swap = trace(c) & 1

    def place_out(s, _):
        for hg in range(4):
            for t in range(12):
                b, m = divmod(t, 3)
                rows = pl.ds(pl.multiple_of(64 * b + 16 * s, 16), 16)
                dev = 2 * (4 * s + hg) + lax.rem(t + swap, 2)
                o_ref[0, 0, rows, (3 * hg + m) * HD : (3 * hg + m + 1) * HD] = xro[dev, t // 2]
        return 0

    lax.fori_loop(0, 4, place_out, 0)
    for a in range(3):
        x_drain(xs.at[a], a)
    x_drain(xso, 3)
    for ring in rings:
        for a in range(3):
            on_sources(ring, functools.partial(z_sent, a, ring))
        pl.when(ring.works)(functools.partial(z_returned, ring))


def packed(cid, plan, clip_shape, route, arrays):
    total = capacity(plan)[-1]
    rows = (total + 1023) // 1024 * 8
    bf = jnp.bfloat16
    smem = pl.BlockSpec(memory_space=pltpu.SMEM)
    exchange = []
    for sources, (_, count, slots) in zip((16, 8, 4), plan):
        exchange.append(pltpu.VMEM((3, count, slots, TILE, HD), bf))
        exchange.append(pltpu.VMEM((3, sources, slots, TILE, HD), bf))
        exchange.append(pltpu.VMEM((sources, slots, TILE, HD), bf))
    n_blocks = max(-(-slots // (16 // sources)) for sources, (_, _, slots) in zip((16, 8, 4), plan))
    return pl.pallas_call(
        functools.partial(kernel, plan),
        out_shape=jax.ShapeDtypeStruct(arrays[0].shape, bf),
        in_specs=[smem] * 2 + [pl.BlockSpec(memory_space=pl.ANY)] * 5,
        out_specs=pl.BlockSpec(memory_space=pltpu.VMEM),
        scratch_shapes=[
            pltpu.VMEM((5, 256, 12 * HD), bf),
            pltpu.VMEM((3, 32, 6, TILE, HD), bf),
            pltpu.VMEM((32, 6, TILE, HD), bf),
            pltpu.VMEM((32, 6, TILE, HD), bf),
            pltpu.VMEM((32, 6, TILE, HD), bf),
            *exchange,
            pltpu.VMEM((3, n_blocks, 256, 256), bf),
            pltpu.VMEM((3, 256, 256), jnp.float32),
            pltpu.VMEM((total + 1, TILE, HD), bf),
            pltpu.VMEM((32, 6, TILE, HD), bf),
            pltpu.VMEM((32, 6, TILE, HD), bf),
            pltpu.VMEM((2, rows, 128), jnp.int32),
            pltpu.SMEM((2, rows, 128), jnp.int32),
            pltpu.SMEM((32,), jnp.int32),
            pltpu.SMEM((32,), jnp.int32),
            pltpu.SMEM((192,), jnp.int32),
            pltpu.SemaphoreType.DMA((5,)),
            pltpu.SemaphoreType.DMA((4,)),
            pltpu.SemaphoreType.DMA((4,)),
            pltpu.SemaphoreType.DMA((4,)),
            pltpu.SemaphoreType.DMA((12,)),
            pltpu.SemaphoreType.DMA((12,)),
            pltpu.SemaphoreType.DMA((12,)),
            pltpu.SemaphoreType.DMA((1,)),
        ],
        compiler_params=pltpu.CompilerParams(
            collective_id=cid, has_side_effects=True, vmem_limit_bytes=56 * 1024 * 1024
        ),
    )(clip_shape, route, *arrays)


def plan_of(clip_shape):
    frames, patches = clip_shape.T[:1], clip_shape.T[1:]
    kind = jnp.arange(6, dtype=jnp.int32)[:, None]
    clips = jnp.arange(32, dtype=jnp.int32)[None, :]
    units = (3 * (patches >> 6) + 1 - ((kind + clips) & 1)) >> 1
    needed = jnp.sum(jnp.where(frames >= (16 >> (kind >> 1)), units, 0), axis=1)
    over = 0
    for plan in PLANS:
        a, b, d = capacity(plan)
        at = jnp.arange(6, dtype=jnp.int32) >> 1
        held = jnp.where(at == 0, a, jnp.where(at == 1, b, d))
        over = over + (needed > held).astype(jnp.int32)
    return jnp.max(over)


def body(query_sp, key_sp, value_sp, query_tm, key_tm, clip_shape, route):
    choice = plan_of(clip_shape)

    def run(i, *args):
        arrays, (shape, way) = args[:5], args[5:]
        return packed(i, PLANS[i], shape.T, way, arrays)

    branches = [functools.partial(run, i) for i in range(len(PLANS))] + [general]
    return lax.switch(
        choice, branches, query_sp, key_sp, value_sp, query_tm, key_tm, clip_shape, route
    )


def solution(mesh):
    in_specs = (
        P("grp", "seq", None, None),
        P("grp", "seq", None, None),
        P("grp", "seq", None, None),
        P("grp", "seq", None, None),
        P("grp", "seq", None, None),
        P(),
        P(),
    )
    out_specs = P("grp", "seq", None, None)
    return jax.shard_map(body, mesh=mesh, in_specs=in_specs, out_specs=out_specs, check_vma=False)
```

profile of v0, /device:TPU:1, one launch (start us, length us, event | category | flops | bytes accessed | tf_op | source)
XLA Modules:
  0.0 109.9 jit_solution(8846921683335546024)
XLA Ops:
  0.0 0.8 slice_bitcast_fusion
  0.8 0.2 select_reduce_fusion
  1.0 0.6 fusion.26
  2.2 106.7 %conditional.1 = (bf16[1,1,256,1536]{3,2,1,0:T(8,128)(2,1)S(1)}) conditional(s32[]{:T(128)} %clamp.3, (s32[32,2]{0,1:T(2,128)}, s32[32]{0:T(128)}, bf16[1,1,256,1536]{3,2,1,0:T(8,128)(2,1)}, bf16[1,1,256,1536]{3,2,1,0:T(8,128)(2,1)}, bf16[1,1,256,1536]{3,2,1,0:T(8,128)(2,1)}, ...), branch_computations={%region_2.3_spmd, %region_3.4_spmd, %region_4.5_spmd, %region_5.10... | conditional | flops 436372544 | bytes 101109008 | solution.py:518
  2.3 106.3 %branch_0_fun.1 = bf16[1,1,256,1536]{3,2,1,0:T(8,128)(2,1)S(1)} custom-call(s32[2,32]{1,0:T(2,128)} %bitcast.64, s32[32]{0:T(128)} %get-tuple-element.66.route_ref, bf16[1,1,256,1536]{3,2,1,0:T(8,128)(2,1)} %get-tuple-element.68.q_hbm, bf16[1,1,256,1536]{3,2,1,0:T(8,128)(2,1)} %get-tuple-element.69.k_hbm, bf16[1,1,256,1536]{3,2,1,0:T(8,128)(2,1)} %get-tuple-element.70.v_hbm, ...), custom_call_target="tpu_custom_call" | custom-call | tf_op jit(solution)/shard_map/cond/branch_0_fun/pallas_call | solution.py:458
  109.0 0.9 copy.86
  (1 shorter events, 0.0 us)
where the time goes:
time: 110 us
  Pallas kernels  106 us (96%)
  other arithmetic  1.59 us (1%)
    pallas_call x1, Pallas kernels, packed(): pl.pallas_call(functools.partial(kernel, plan), out_shape=jax.ShapeDtypeS...  106 us

commit v1 on v0

--- a/solution.py
+++ b/solution.py
@@ -12,9 +12,9 @@
 MESH = pl.DeviceIdType.MESH
 NEG = -1e30
 PLANS = (
-    ((6, 11, 5), (3, 2, 17), (1, 2, 21)),
-    ((6, 12, 6), (3, 2, 19), (2, 1, 34)),
-    ((4, 13, 7), (2, 2, 18), (1, 1, 23)),
+    ((6, 12, 2), (3, 2, 10), (1, 2, 11)),
+    ((6, 12, 3), (3, 2, 9), (2, 1, 18)),
+    ((5, 14, 3), (3, 2, 11), (1, 2, 8)),
 )
 
 
@@ -115,15 +115,17 @@
 def kernel(
     plan, shape_ref, route_ref,
     q_hbm, k_hbm, v_hbm, qt_hbm, kt_hbm, o_ref,
-    inp, xs, xr0, xr1, xr2, zs16, zq16, oz16, zs8, zq8, oz8, zs4, zq4, oz4, wts, bias, zr, xso, xro,
-    table, slot_ref, first, units, out_tab,
-    in_sem, xss, xrs, xls, zss, zrs, zls, tab_sem,
+    inp, xs, *refs,
 ):
     total = capacity(plan)[-1]
+    xr, refs = (refs[0:3], refs[3:6]), refs[6:]
+    exchange, refs = (refs[0:9], refs[9:18]), refs[18:]
+    wts, bias, zr0, zr1, xso, xro, table, slot_ref, first, units, out_tab, *refs = refs
+    in_sem, xss, xrs, xls, zss, zrs, zls, tab_sem = refs
+    zr = (zr0, zr1)
     c = lax.axis_index("grp")
     z = lax.axis_index("seq")
     core = lax.rem(c, 2)
-    xr = (xr0, xr1, xr2)
     barrier = pltpu.get_barrier_semaphore()
 
     def greet_x(d, _):
@@ -143,6 +145,9 @@
     ]
     for load in loads:
         load.start()
+
+    def half_of(i, clip):
+        return (i + (clip >> 1)) & 1
 
     def pack(a):
         def group(s, _):
@@ -152,7 +157,7 @@
                     rows = pl.ds(pl.multiple_of(64 * b + 16 * s, 16), 16)
                     lanes = pl.ds((3 * hg + m) * HD, HD)
                     dev = 2 * (4 * s + hg) + lax.rem(t + core, 2)
-                    xs[a, dev, t // 2] = inp[a, rows, lanes]
+                    xs[a, half_of(t // 2, c), dev, t // 4] = inp[a, rows, lanes]
             return 0
 
         lax.fori_loop(0, 4, group, 0)
@@ -184,42 +189,46 @@
     loads[0].wait()
     pack(0)
     pl.semaphore_wait(barrier, 46)
-    x_send(xs.at[0], xr[0], 0)
+    for h in range(2):
+        x_send(xs.at[0, h], xr[h][0], h)
     loads[1].wait()
     pack(1)
-    x_send(xs.at[1], xr[1], 1)
-
-    def count_units(clip, sums):
-        frames = shape_ref[0, clip]
-        count = (3 * (shape_ref[1, clip] >> 6) + 1 - ((core + clip) & 1)) >> 1
-        units[clip] = count
-        is16, is8 = frames == 16, frames == 8
-        first[clip] = jnp.where(is16, sums[0], jnp.where(is8, sums[1], sums[2]))
-        return (
-            sums[0] + jnp.where(is16, count, 0),
-            sums[1] + jnp.where(is8, count, 0),
-            sums[2] + jnp.where(is16 | is8, 0, count),
-        )
-
+    for h in range(2):
+        x_send(xs.at[1, h], xr[h][1], 2 + h)
+
+    row = lax.broadcasted_iota(jnp.int32, table.shape[2:], 0)
+    lane = lax.broadcasted_iota(jnp.int32, table.shape[2:], 1)
+    place = 128 * row + lane
     zero = jnp.int32(0)
-    n16, n8, _ = lax.fori_loop(0, 32, count_units, (zero, zero, zero))
-
-    row = lax.broadcasted_iota(jnp.int32, table.shape[1:], 0)
-    lane = lax.broadcasted_iota(jnp.int32, table.shape[1:], 1)
-    place = 128 * row + lane
-
-    def find_slots(clip, found):
-        unit, count = found
-        frames = shape_ref[0, clip]
-        start = first[clip] + jnp.where(frames == 16, 0, jnp.where(frames == 8, n16, n16 + n8))
-        first[clip] = start
-        inner = place - start
-        hit = (inner >= 0) & (inner < units[clip])
-        return jnp.where(hit, inner + 6 * clip, unit), jnp.where(hit, frames, count)
-
-    unit, count = lax.fori_loop(0, 32, find_slots, (jnp.zeros_like(place), jnp.full_like(place, 16)))
-    table[0] = unit
-    table[1] = count
+    for h in range(2):
+
+        def count_units(clip, sums):
+            frames = shape_ref[0, clip]
+            count = (3 * (shape_ref[1, clip] >> 6) + 1 - ((core + clip) & 1)) >> 1
+            count = (count + 1 - ((h + (clip >> 1)) & 1)) >> 1
+            units[h, clip] = count
+            is16, is8 = frames == 16, frames == 8
+            first[h, clip] = jnp.where(is16, sums[0], jnp.where(is8, sums[1], sums[2]))
+            return (
+                sums[0] + jnp.where(is16, count, 0),
+                sums[1] + jnp.where(is8, count, 0),
+                sums[2] + jnp.where(is16 | is8, 0, count),
+            )
+
+        n16, n8, _ = lax.fori_loop(0, 32, count_units, (zero, zero, zero))
+
+        def find_slots(clip, found):
+            unit, count = found
+            frames = shape_ref[0, clip]
+            start = first[h, clip] + jnp.where(frames == 16, 0, jnp.where(frames == 8, n16, n16 + n8))
+            first[h, clip] = start
+            inner = place - start
+            hit = (inner >= 0) & (inner < units[h, clip])
+            return jnp.where(hit, inner + 3 * clip, unit), jnp.where(hit, frames, count)
+
+        unit, count = lax.fori_loop(0, 32, find_slots, (jnp.zeros_like(place), jnp.full_like(place, 16)))
+        table[h, 0] = unit
+        table[h, 1] = count
     to_smem = pltpu.make_async_copy(table, slot_ref, tab_sem.at[0])
     to_smem.start()
 
@@ -229,7 +238,8 @@
         period = 16 * 2**i
         same = (row_id & (period - 1)) == (col_id & (period - 1))
         bias[i] = jnp.where(same, 0.0, NEG)
-    zr[total] = jnp.zeros((TILE, HD), jnp.bfloat16)
+    for h in range(2):
+        zr[h][total] = jnp.zeros((TILE, HD), jnp.bfloat16)
 
     for i in (2, 3, 4):
         loads[i].wait()
@@ -248,25 +258,27 @@
                 t = 3 * b + m
                 for s in range(4):
                     dev = 2 * (4 * s + hg) + lax.rem(t + core, 2)
-                    xs[2, dev, t // 2] = out[64 * b + 16 * s : 64 * b + 16 * s + 16]
+                    xs[2, half_of(t // 2, c), dev, t // 4] = out[64 * b + 16 * s : 64 * b + 16 * s + 16]
         return 0
 
     lax.fori_loop(0, 4, heads, 0)
-    x_send(xs.at[2], xr[2], 2)
+    for h in range(2):
+        x_send(xs.at[2, h], xr[h][2], 4 + h)
     to_smem.wait()
 
     class Ring:
-        def __init__(self, kind, sources, send, land, back):
-            self.kind, self.sources, self.send, self.land, self.back = kind, sources, send, land, back
+        def __init__(self, half, kind, send, land, back):
+            self.half, self.kind, self.sources, self.sem = half, kind, 16 >> kind, 12 * half + kind
+            self.send, self.land, self.back = send, land, back
             self.start, self.count, self.slots = plan[kind]
             self.off = capacity(plan)[kind] - self.count * self.slots
             self.place = lax.rem(z - self.start + 16, 16)
             self.works = self.place < self.count
 
-    rings = (Ring(0, 16, zs16, zq16, oz16), Ring(1, 8, zs8, zq8, oz8), Ring(2, 4, zs4, zq4, oz4))
-
-    def entry(kind, r):
-        return slot_ref[kind, r >> 7, r & 127]
+    halves = [[Ring(h, kind, *exchange[h][3 * kind : 3 * kind + 3]) for kind in range(3)] for h in range(2)]
+
+    def entry(half, kind, r):
+        return slot_ref[half, kind, r >> 7, r & 127]
 
     def on_sources(ring, run):
         if ring.sources == 16:
@@ -275,14 +287,14 @@
             pl.when(z < ring.sources)(run)
 
     def z_send(a, ring):
-        i = 3 * a + ring.kind
+        i = 3 * a + ring.sem
 
         def one(d, _):
             j = lax.rem(z + d, ring.count)
             dev = lax.rem(ring.start + j, 16)
             for k in range(ring.slots):
-                index = entry(0, ring.off + j * ring.slots + k)
-                ring.send[a, j, k] = xr[a][index // 6, lax.rem(index, 6)]
+                index = entry(ring.half, 0, ring.off + j * ring.slots + k)
+                ring.send[a, j, k] = xr[ring.half][a][index // 3, lax.rem(index, 3)]
 
             @pl.when(dev != z)
             def _():
@@ -300,7 +312,7 @@
         lax.fori_loop(0, ring.count, one, 0)
 
     def z_sent(a, ring):
-        i = 3 * a + ring.kind
+        i = 3 * a + ring.sem
         for mine in (0, 1):
             if ring.count > mine:
 
@@ -310,16 +322,17 @@
                     pltpu.make_async_copy(part, part, zss.at[i]).wait()
 
     def z_wait(a, ring):
-        i = 3 * a + ring.kind
+        i = 3 * a + ring.sem
         part = ring.land.at[a, pl.ds(0, ring.sources - 1)]
         pltpu.make_async_copy(part, part, zrs.at[i]).wait()
         one = ring.land.at[a, 0]
         pltpu.make_async_copy(one, one, zls.at[i]).wait()
 
     for a in range(3):
-        x_wait(xs.at[a], xr[a], a)
-        for ring in rings:
-            on_sources(ring, functools.partial(z_send, a, ring))
+        for h in range(2):
+            x_wait(xs.at[a, h], xr[h][a], 2 * a + h)
+            for ring in halves[h]:
+                on_sources(ring, functools.partial(z_send, a, ring))
 
     def trace(group):
         for b in reversed(range(5)):
@@ -329,15 +342,16 @@
 
     def route_units(group, _):
         clip = trace(group)
-        start = first[clip]
-        count = jnp.where(z < shape_ref[0, clip], units[clip], 0)
-        for i in range(6):
-            out_tab[group * 6 + i] = jnp.where(i < count, start + i, total)
+        for h in range(2):
+            start = first[h, clip]
+            count = jnp.where(z < shape_ref[0, clip], units[h, clip], 0)
+            for i in range(3):
+                out_tab[h, group * 3 + i] = jnp.where(i < count, start + i, total)
         return 0
 
     lax.fori_loop(0, 32, route_units, 0)
 
-    for ring in rings:
+    for ring in halves[0] + halves[1]:
         step = 16 // ring.sources
         ring.blocks = [(k, min(step, ring.slots - k), k // step) for k in range(0, ring.slots, step)]
 
@@ -361,24 +375,24 @@
                 lane = lax.broadcasted_iota(jnp.int32, (1, rows), 1)
                 frame = lane // (n * TILE)
                 spot = ring.off + ring.place * ring.slots + k
-                count = entry(1, spot)
+                count = entry(ring.half, 1, spot)
                 if n == 2:
-                    count = jnp.where((lane // TILE) % 2 == 0, count, entry(1, spot + 1))
+                    count = jnp.where((lane // TILE) % 2 == 0, count, entry(ring.half, 1, spot + 1))
                 scores = scores + jnp.where(frame < count, 0.0, NEG)
-            wts[ring.kind, at, :rows, :rows] = softmax_weights(scores)
+            wts[ring.half, ring.kind, at, :rows, :rows] = softmax_weights(scores)
 
     def z_values(ring):
         z_wait(2, ring)
         for k, n, at in ring.blocks:
             rows = ring.sources * n * TILE
             out = jnp.dot(
-                wts[ring.kind, at, :rows, :rows], block(ring, 2, k, n), preferred_element_type=jnp.float32
+                wts[ring.half, ring.kind, at, :rows, :rows], block(ring, 2, k, n), preferred_element_type=jnp.float32
             ).astype(jnp.bfloat16)
             out = out.reshape(ring.sources, n, TILE, HD)
             for j in range(n):
                 ring.back[:, k + j] = out[:, j]
-        i = 9 + ring.kind
-        home = zr.at[pl.ds(ring.off + ring.place * ring.slots, ring.slots)]
+        i = 9 + ring.sem
+        home = zr[ring.half].at[pl.ds(ring.off + ring.place * ring.slots, ring.slots)]
 
         def one(d, _):
             dev = lax.rem(z + d, ring.sources)
@@ -392,13 +406,13 @@
         pltpu.make_async_copy(ring.back.at[z], home, zls.at[i]).start()
 
     def z_home(ring):
-        i = 9 + ring.kind
+        i = 9 + ring.sem
         for mine in (0, 1):
 
             @pl.when(ring.works if mine else jnp.logical_not(ring.works))
             def _():
                 if ring.count > mine:
-                    part = zr.at[pl.ds(ring.off, (ring.count - mine) * ring.slots)]
+                    part = zr[ring.half].at[pl.ds(ring.off, (ring.count - mine) * ring.slots)]
                     pltpu.make_async_copy(part, part, zrs.at[i]).wait()
                 if mine:
                     one = ring.back.at[0]
@@ -406,42 +420,47 @@
 
     def z_returned(ring):
         part = ring.back.at[pl.ds(0, ring.sources - 1)]
-        pltpu.make_async_copy(part, part, zss.at[9 + ring.kind]).wait()
-
-    for ring in rings:
-        pl.when(ring.works)(functools.partial(z_weights, ring))
-    for ring in rings:
-        pl.when(ring.works)(functools.partial(z_values, ring))
-    for ring in rings:
-        on_sources(ring, functools.partial(z_home, ring))
-
-    def collect(dev, _):
-        for i in range(6):
-            xso[dev, i] = zr[out_tab[dev * 6 + i]]
-        return 0
-
-    lax.fori_loop(0, 32, collect, 0)
-    x_send(xso, xro, 3)
-    x_wait(xso, xro, 3)
-    swap = trace(c) & 1
+        pltpu.make_async_copy(part, part, zss.at[9 + ring.sem]).wait()
+
+    for rings in halves:
+        for ring in rings:
+            pl.when(ring.works)(functools.partial(z_weights, ring))
+        for ring in rings:
+            pl.when(ring.works)(functools.partial(z_values, ring))
+
+    for h in range(2):
+        for ring in halves[h]:
+            on_sources(ring, functools.partial(z_home, ring))
+
+        def collect(dev, _):
+            for i in range(3):
+                xso[h, dev, i] = zr[h][out_tab[h, dev * 3 + i]]
+            return 0
+
+        lax.fori_loop(0, 32, collect, 0)
+        x_send(xso.at[h], xro.at[h], 6 + h)
+    for h in range(2):
+        x_wait(xso.at[h], xro.at[h], 6 + h)
+    clip = trace(c)
 
     def place_out(s, _):
         for hg in range(4):
             for t in range(12):
                 b, m = divmod(t, 3)
                 rows = pl.ds(pl.multiple_of(64 * b + 16 * s, 16), 16)
-                dev = 2 * (4 * s + hg) + lax.rem(t + swap, 2)
-                o_ref[0, 0, rows, (3 * hg + m) * HD : (3 * hg + m + 1) * HD] = xro[dev, t // 2]
+                dev = 2 * (4 * s + hg) + ((t + clip) & 1)
+                o_ref[0, 0, rows, (3 * hg + m) * HD : (3 * hg + m + 1) * HD] = xro[half_of(t // 2, clip), dev, t // 4]
         return 0
 
     lax.fori_loop(0, 4, place_out, 0)
-    for a in range(3):
-        x_drain(xs.at[a], a)
-    x_drain(xso, 3)
-    for ring in rings:
+    for h in range(2):
         for a in range(3):
-            on_sources(ring, functools.partial(z_sent, a, ring))
-        pl.when(ring.works)(functools.partial(z_returned, ring))
+            x_drain(xs.at[a, h], 2 * a + h)
+        x_drain(xso.at[h], 6 + h)
+        for ring in halves[h]:
+            for a in range(3):
+                on_sources(ring, functools.partial(z_sent, a, ring))
+            pl.when(ring.works)(functools.partial(z_returned, ring))
 
 
 def packed(cid, plan, clip_shape, route, arrays):
@@ -462,28 +481,24 @@
         out_specs=pl.BlockSpec(memory_space=pltpu.VMEM),
         scratch_shapes=[
             pltpu.VMEM((5, 256, 12 * HD), bf),
-            pltpu.VMEM((3, 32, 6, TILE, HD), bf),
-            pltpu.VMEM((32, 6, TILE, HD), bf),
-            pltpu.VMEM((32, 6, TILE, HD), bf),
-            pltpu.VMEM((32, 6, TILE, HD), bf),
+            pltpu.VMEM((3, 2, 32, 3, TILE, HD), bf),
+            *[pltpu.VMEM((32, 3, TILE, HD), bf)] * 6,
             *exchange,
-            pltpu.VMEM((3, n_blocks, 256, 256), bf),
+            *exchange,
+            pltpu.VMEM((2, 3, n_blocks, 256, 256), bf),
             pltpu.VMEM((3, 256, 256), jnp.float32),
             pltpu.VMEM((total + 1, TILE, HD), bf),
-            pltpu.VMEM((32, 6, TILE, HD), bf),
-            pltpu.VMEM((32, 6, TILE, HD), bf),
-            pltpu.VMEM((2, rows, 128), jnp.int32),
-            pltpu.SMEM((2, rows, 128), jnp.int32),
-            pltpu.SMEM((32,), jnp.int32),
-            pltpu.SMEM((32,), jnp.int32),
-            pltpu.SMEM((192,), jnp.int32),
+            pltpu.VMEM((total + 1, TILE, HD), bf),
+            pltpu.VMEM((2, 32, 3, TILE, HD), bf),
+            pltpu.VMEM((2, 32, 3, TILE, HD), bf),
+            pltpu.VMEM((2, 2, rows, 128), jnp.int32),
+            pltpu.SMEM((2, 2, rows, 128), jnp.int32),
+            pltpu.SMEM((2, 32), jnp.int32),
+            pltpu.SMEM((2, 32), jnp.int32),
+            pltpu.SMEM((2, 96), jnp.int32),
             pltpu.SemaphoreType.DMA((5,)),
-            pltpu.SemaphoreType.DMA((4,)),
-            pltpu.SemaphoreType.DMA((4,)),
-            pltpu.SemaphoreType.DMA((4,)),
-            pltpu.SemaphoreType.DMA((12,)),
-            pltpu.SemaphoreType.DMA((12,)),
-            pltpu.SemaphoreType.DMA((12,)),
+            *[pltpu.SemaphoreType.DMA((8,))] * 3,
+            *[pltpu.SemaphoreType.DMA((24,))] * 3,
             pltpu.SemaphoreType.DMA((1,)),
         ],
         compiler_params=pltpu.CompilerParams(
@@ -494,14 +509,15 @@
 
 def plan_of(clip_shape):
     frames, patches = clip_shape.T[:1], clip_shape.T[1:]
-    kind = jnp.arange(6, dtype=jnp.int32)[:, None]
+    kind = jnp.arange(12, dtype=jnp.int32)[:, None]
     clips = jnp.arange(32, dtype=jnp.int32)[None, :]
     units = (3 * (patches >> 6) + 1 - ((kind + clips) & 1)) >> 1
-    needed = jnp.sum(jnp.where(frames >= (16 >> (kind >> 1)), units, 0), axis=1)
+    units = (units + 1 - (((kind >> 1) + (clips >> 1)) & 1)) >> 1
+    needed = jnp.sum(jnp.where(frames >= (16 >> (kind >> 2)), units, 0), axis=1)
     over = 0
     for plan in PLANS:
         a, b, d = capacity(plan)
-        at = jnp.arange(6, dtype=jnp.int32) >> 1
+        at = jnp.arange(12, dtype=jnp.int32) >> 2
         held = jnp.where(at == 0, a, jnp.where(at == 1, b, d))
         over = over + (needed > held).astype(jnp.int32)
     return jnp.max(over)

time: 110 us -> 102 us (0.927)
  Pallas kernels: 106 us -> 97.8 us
    pallas_call x1, Pallas kernels: 106 us -> 97.8 us  [packed(): pl.pallas_call(functools.partial(kernel, plan), out_shape=jax.ShapeDtypeS...]
where the time goes in v1:
time: 102 us; the launch traced here: 101 us
  Pallas kernels  97.8 us (96%)
  other arithmetic  1.6 us (2%)
    pallas_call x1, Pallas kernels, packed(): pl.pallas_call(functools.partial(kernel, plan), out_shape=jax.ShapeDtypeS...  97.8 us

profile of v1, /device:TPU:1, one launch (start us, length us, event | category | flops | bytes accessed | tf_op | source)
XLA Modules:
  0.0 101.5 jit_solution(2642028367783565418)
XLA Ops:
  0.0 0.8 slice_bitcast_fusion
  0.8 0.2 select_reduce_fusion
  1.0 0.6 fusion.26
  2.3 98.4 %conditional.1 = (bf16[1,1,256,1536]{3,2,1,0:T(8,128)(2,1)S(1)}) conditional(s32[]{:T(128)} %clamp.3, (s32[32,2]{0,1:T(2,128)}, s32[32]{0:T(128)}, bf16[1,1,256,1536]{3,2,1,0:T(8,128)(2,1)}, bf16[1,1,256,1536]{3,2,1,0:T(8,128)(2,1)}, bf16[1,1,256,1536]{3,2,1,0:T(8,128)(2,1)}, ...), branch_computations={%region_2.3_spmd, %region_3.4_spmd, %region_4.5_spmd, %region_5.10... | conditional | flops 436372544 | bytes 101109008 | solution.py:534
  2.3 97.8 %branch_0_fun.1 = bf16[1,1,256,1536]{3,2,1,0:T(8,128)(2,1)S(1)} custom-call(s32[2,32]{1,0:T(2,128)} %bitcast.64, s32[32]{0:T(128)} %get-tuple-element.66.route_ref, bf16[1,1,256,1536]{3,2,1,0:T(8,128)(2,1)} %get-tuple-element.68.q_hbm, bf16[1,1,256,1536]{3,2,1,0:T(8,128)(2,1)} %get-tuple-element.69.k_hbm, bf16[1,1,256,1536]{3,2,1,0:T(8,128)(2,1)} %get-tuple-element.70.v_hbm, ...), custom_call_target="tpu_custom_call" | custom-call | tf_op jit(solution)/shard_map/cond/branch_0_fun/pallas_call | solution.py:477
  100.6 0.9 copy.86
  (2 shorter events, 0.0 us)

commit v2 on v1

--- a/solution.py
+++ b/solution.py
@@ -191,11 +191,6 @@
     pl.semaphore_wait(barrier, 46)
     for h in range(2):
         x_send(xs.at[0, h], xr[h][0], h)
-    loads[1].wait()
-    pack(1)
-    for h in range(2):
-        x_send(xs.at[1, h], xr[h][1], 2 + h)
-
     row = lax.broadcasted_iota(jnp.int32, table.shape[2:], 0)
     lane = lax.broadcasted_iota(jnp.int32, table.shape[2:], 1)
     place = 128 * row + lane
@@ -231,6 +226,82 @@
         table[h, 1] = count
     to_smem = pltpu.make_async_copy(table, slot_ref, tab_sem.at[0])
     to_smem.start()
+
+    loads[1].wait()
+    pack(1)
+    for h in range(2):
+        x_send(xs.at[1, h], xr[h][1], 2 + h)
+
+    class Ring:
+        def __init__(self, half, kind, send, land, back):
+            self.half, self.kind, self.sources, self.sem = half, kind, 16 >> kind, 12 * half + kind
+            self.send, self.land, self.back = send, land, back
+            self.start, self.count, self.slots = plan[kind]
+            self.off = capacity(plan)[kind] - self.count * self.slots
+            self.place = lax.rem(z - self.start + 16, 16)
+            self.works = self.place < self.count
+
+    halves = [[Ring(h, kind, *exchange[h][3 * kind : 3 * kind + 3]) for kind in range(3)] for h in range(2)]
+
+    def entry(half, kind, r):
+        return slot_ref[half, kind, r >> 7, r & 127]
+
+    def on_sources(ring, run):
+        if ring.sources == 16:
+            run()
+        else:
+            pl.when(z < ring.sources)(run)
+
+    def z_send(a, ring):
+        i = 3 * a + ring.sem
+
+        def one(d, _):
+            j = lax.rem(z + d, ring.count)
+            dev = lax.rem(ring.start + j, 16)
+            for k in range(ring.slots):
+                index = entry(ring.half, 0, ring.off + j * ring.slots + k)
+                ring.send[a, j, k] = xr[ring.half][a][index // 3, lax.rem(index, 3)]
+
+            @pl.when(dev != z)
+            def _():
+                pltpu.make_async_remote_copy(
+                    src_ref=ring.send.at[a, j], dst_ref=ring.land.at[a, z], send_sem=zss.at[i], recv_sem=zrs.at[i],
+                    device_id={"seq": dev}, device_id_type=MESH,
+                ).start()
+
+            @pl.when(dev == z)
+            def _():
+                pltpu.make_async_copy(ring.send.at[a, j], ring.land.at[a, z], zls.at[i]).start()
+
+            return 0
+
+        lax.fori_loop(0, ring.count, one, 0)
+
+    def z_sent(a, ring):
+        i = 3 * a + ring.sem
+        for mine in (0, 1):
+            if ring.count > mine:
+
+                @pl.when(ring.works if mine else jnp.logical_not(ring.works))
+                def _():
+                    part = ring.send.at[a, pl.ds(0, ring.count - mine)]
+                    pltpu.make_async_copy(part, part, zss.at[i]).wait()
+
+    def z_wait(a, ring):
+        i = 3 * a + ring.sem
+        part = ring.land.at[a, pl.ds(0, ring.sources - 1)]
+        pltpu.make_async_copy(part, part, zrs.at[i]).wait()
+        one = ring.land.at[a, 0]
+        pltpu.make_async_copy(one, one, zls.at[i]).wait()
+
+    def pass_on(a):
+        for h in range(2):
+            x_wait(xs.at[a, h], xr[h][a], 2 * a + h)
+            for ring in halves[h]:
+                on_sources(ring, functools.partial(z_send, a, ring))
+
+    to_smem.wait()
+    pass_on(0)
 
     row_id = lax.broadcasted_iota(jnp.int32, (256, 256), 0)
     col_id = lax.broadcasted_iota(jnp.int32, (256, 256), 1)
@@ -264,75 +335,9 @@
     lax.fori_loop(0, 4, heads, 0)
     for h in range(2):
         x_send(xs.at[2, h], xr[h][2], 4 + h)
-    to_smem.wait()
-
-    class Ring:
-        def __init__(self, half, kind, send, land, back):
-            self.half, self.kind, self.sources, self.sem = half, kind, 16 >> kind, 12 * half + kind
-            self.send, self.land, self.back = send, land, back
-            self.start, self.count, self.slots = plan[kind]
-            self.off = capacity(plan)[kind] - self.count * self.slots
-            self.place = lax.rem(z - self.start + 16, 16)
-            self.works = self.place < self.count
-
-    halves = [[Ring(h, kind, *exchange[h][3 * kind : 3 * kind + 3]) for kind in range(3)] for h in range(2)]
-
-    def entry(half, kind, r):
-        return slot_ref[half, kind, r >> 7, r & 127]
-
-    def on_sources(ring, run):
-        if ring.sources == 16:
-            run()
-        else:
-            pl.when(z < ring.sources)(run)
-
-    def z_send(a, ring):
-        i = 3 * a + ring.sem
-
-        def one(d, _):
-            j = lax.rem(z + d, ring.count)
-            dev = lax.rem(ring.start + j, 16)
-            for k in range(ring.slots):
-                index = entry(ring.half, 0, ring.off + j * ring.slots + k)
-                ring.send[a, j, k] = xr[ring.half][a][index // 3, lax.rem(index, 3)]
-
-            @pl.when(dev != z)
-            def _():
-                pltpu.make_async_remote_copy(
-                    src_ref=ring.send.at[a, j], dst_ref=ring.land.at[a, z], send_sem=zss.at[i], recv_sem=zrs.at[i],
-                    device_id={"seq": dev}, device_id_type=MESH,
-                ).start()
-
-            @pl.when(dev == z)
-            def _():
-                pltpu.make_async_copy(ring.send.at[a, j], ring.land.at[a, z], zls.at[i]).start()
-
-            return 0
-
-        lax.fori_loop(0, ring.count, one, 0)
-
-    def z_sent(a, ring):
-        i = 3 * a + ring.sem
-        for mine in (0, 1):
-            if ring.count > mine:
-
-                @pl.when(ring.works if mine else jnp.logical_not(ring.works))
-                def _():
-                    part = ring.send.at[a, pl.ds(0, ring.count - mine)]
-                    pltpu.make_async_copy(part, part, zss.at[i]).wait()
-
-    def z_wait(a, ring):
-        i = 3 * a + ring.sem
-        part = ring.land.at[a, pl.ds(0, ring.sources - 1)]
-        pltpu.make_async_copy(part, part, zrs.at[i]).wait()
-        one = ring.land.at[a, 0]
-        pltpu.make_async_copy(one, one, zls.at[i]).wait()
-
-    for a in range(3):
-        for h in range(2):
-            x_wait(xs.at[a, h], xr[h][a], 2 * a + h)
-            for ring in halves[h]:
-                on_sources(ring, functools.partial(z_send, a, ring))
+
+    pass_on(1)
+    pass_on(2)
 
     def trace(group):
         for b in reversed(range(5)):

time: 102 us -> 110 us (1.078)
  Pallas kernels: 97.8 us -> 106 us
    pallas_call x1, Pallas kernels: 97.8 us -> 106 us  [packed(): pl.pallas_call(functools.partial(kernel, plan), out_shape=jax.ShapeDtypeS...]
where the time goes in v2:
time: 110 us; the launch traced here: 109 us
  Pallas kernels  106 us (96%)
  other arithmetic  1.6 us (1%)
    pallas_call x1, Pallas kernels, packed(): pl.pallas_call(functools.partial(kernel, plan), out_shape=jax.ShapeDtypeS...  106 us

profile of v2, /device:TPU:1, one launch (start us, length us, event | category | flops | bytes accessed | tf_op | source)
XLA Modules:
  0.0 109.3 jit_solution(8433331083966865713)
XLA Ops:
  0.0 0.8 slice_bitcast_fusion
  0.8 0.2 select_reduce_fusion
  1.0 0.6 fusion.26
  2.3 106.1 %conditional.1 = (bf16[1,1,256,1536]{3,2,1,0:T(8,128)(2,1)S(1)}) conditional(s32[]{:T(128)} %clamp.3, (s32[32,2]{0,1:T(2,128)}, s32[32]{0:T(128)}, bf16[1,1,256,1536]{3,2,1,0:T(8,128)(2,1)}, bf16[1,1,256,1536]{3,2,1,0:T(8,128)(2,1)}, bf16[1,1,256,1536]{3,2,1,0:T(8,128)(2,1)}, ...), branch_computations={%region_2.3_spmd, %region_3.4_spmd, %region_4.5_spmd, %region_5.10... | conditional | flops 436372544 | bytes 101109008 | solution.py:539
  2.3 105.6 %branch_1_fun.1 = bf16[1,1,256,1536]{3,2,1,0:T(8,128)(2,1)S(1)} custom-call(s32[2,32]{1,0:T(2,128)} %bitcast.65, s32[32]{0:T(128)} %get-tuple-element.74.route_ref, bf16[1,1,256,1536]{3,2,1,0:T(8,128)(2,1)} %get-tuple-element.75.q_hbm, bf16[1,1,256,1536]{3,2,1,0:T(8,128)(2,1)} %get-tuple-element.76.k_hbm, bf16[1,1,256,1536]{3,2,1,0:T(8,128)(2,1)} %get-tuple-element.77.v_hbm, ...), custom_call_target="tpu_custom_call" | custom-call | tf_op jit(solution)/shard_map/cond/branch_1_fun/pallas_call | solution.py:482
  108.4 0.9 copy.86
  (2 shorter events, 0.0 us)
